TPU v7x, 32 devices: a whole 2x2x4 slice. The times are simulated.
32 devices in a mesh: row: 2 (over core), col: 4 (over z), cell: 4 (over y, x).
Axes of the slice: x: 2, y: 2, z: 4, core: 2. Of those that a mesh axis runs over, the one named last changes fastest.
Arguments:
- populations: float32 [16384, 1024], P(('row', 'col'), 'cell'), parts along dimension 1, may hold values from -6 to 6
- source: float32 [16384, 1024], P(('row', 'col'), 'cell'), parts along dimension 1, may hold values from -6 to 6
- loss_rates: float32 [8, 16384], P(None, ('row', 'col')), may hold values from 0.05 to 0.5
- basis_table: float32 [8, 64], replicated, may hold values from 0.25 to 4
- temp_bins: int32 [1024], P('cell'), parts along dimension 0, may hold values from 0 to 63
- rate_blocks: bfloat16 [2, 4, 32, 8, 128, 128], P('row', 'col'), may hold values from -0.09375 to 0.09375
- block_rows: int32 [2, 4, 32], P('row', 'col'), may hold values from 0 to 31, as said below
- block_cols: int32 [2, 4, 32], P('row', 'col'), may hold values from 0 to 63, as said below
- block_count: int32 [2, 4], P('row', 'col'), may hold values from 1 to 32, as said below
Outputs:
- updated: float32 [16384, 1024], P(('row', 'col'), 'cell'), parts along dimension 1
There are 4 independent parts, one for each index of `cell`. A program takes and returns all parts, laid end to end along the dimension named above; an argument that names none is the same for every part. Nothing has to cross between parts.
Inputs may be any that keep to these rules, and one draw needn't show every extreme that they name: The slots of a tile name distinct block positions (block_rows, block_cols); every tile names its first and its last block position among its slots. `block_cols`: paired with block_rows slot by slot. `block_count`: in one index of row, drawn from the seed, every tile has 32 live slots; every other tile has at most 16.
All inputs are finite; a program needn't handle non-finite values.
Results may differ from a plain program's by a relative error of at most 0.002.
Values sent between devices are 32-bit elements; how exact they have to be, the bound alone decides.
A program may use at most 128 MiB of HBM per device.

v0:
```python
import jax
import jax.numpy as jnp
from jax import lax
from jax.sharding import PartitionSpec as P

ITERS = 2


def per_device(
    populations,
    source,
    loss_rates,
    basis_table,
    temp_bins,
    rate_blocks,
    block_rows,
    block_cols,
    block_count,
):
    cell_count = populations.shape[1]
    bin_count = basis_table.shape[1]
    block_size = rate_blocks.shape[-1]
    part_rows = populations.shape[0]
    row_devices = lax.axis_size("row")
    onehot = (temp_bins[None, :] == jnp.arange(bin_count, dtype=jnp.int32)[:, None]).astype(
        jnp.float32
    )
    factors = jnp.dot(basis_table, onehot, precision=lax.Precision.HIGHEST)
    denominator = jnp.einsum("kl,kc->lc", loss_rates, factors, precision=lax.Precision.HIGHEST)
    blocks = rate_blocks[0, 0]
    slot_rows = block_rows[0, 0]
    slot_cols = block_cols[0, 0]
    live_slots = block_count[0, 0]
    for sweep in range(ITERS):
        weighted = (
            factors[:, None, :] * lax.all_gather(populations, "col", axis=0, tiled=True)[None, :, :]
        ).astype(jnp.bfloat16)

        def fetch(slot):
            return lax.dynamic_slice_in_dim(weighted, slot_cols[slot] * block_size, block_size, 1)

        def slot_product(slot):
            return jnp.einsum(
                "kij,kjc->ic", blocks[slot], fetch(slot), preferred_element_type=jnp.float32
            )

        def add_slot(slot, totals):
            row_start = slot_rows[slot] * block_size
            current = lax.dynamic_slice_in_dim(totals, row_start, block_size, 0)
            return lax.dynamic_update_slice_in_dim(
                totals, current + slot_product(slot), row_start, 0
            )

        totals = lax.fori_loop(
            0, live_slots, add_slot, jnp.zeros((row_devices * part_rows, cell_count), jnp.float32)
        )
        coupling = lax.psum_scatter(totals, "row", scatter_dimension=0, tiled=True)
        populations = (source + coupling) / denominator
    return populations


def solution(mesh):
    in_specs = (
        P(("row", "col"), "cell"),
        P(("row", "col"), "cell"),
        P(None, ("row", "col")),
        P(),
        P("cell"),
        P("row", "col", None, None, None, None),
        P("row", "col", None),
        P("row", "col", None),
        P("row", "col"),
    )
    out_specs = P(("row", "col"), "cell")
    return jax.shard_map(
        per_device, mesh=mesh, in_specs=in_specs, out_specs=out_specs, check_vma=False
    )
```

profile of v0, /device:TPU:0, one launch (start us, length us, event | category | flops | bytes accessed | tf_op | source)
XLA Modules:
  0.0 808.1 jit_solution(18271570067454765372)
XLA Ops:
  8.1 153.2 %all-gather.3.cloned.1.call-done = f32[8192,256]{1,0:T(8,128)} async-done(((f32[2048,256]{1,0:T(8,128)}), f32[8192,256]{1,0:T(8,128)}) %all-gather.3.cloned.1.call-update) | async-done | bytes 8388624 | tf_op jit(solution)/shard_map/all_gather | solution.py:36
  161.3 13.6 %multiply_convert_fusion.1 = bf16[8,8192,256]{2,1,0:T(8,128)(2,1)} fusion(f32[8192,256]{1,0:T(8,128)} %all-gather.3.cloned.1.call-done, f32[8,256]{1,0:T(8,128)S(1)} %bitcast.45), kind=kLoop, calls=%fused_computation.17 | loop fusion | flops 33554432 | bytes 41951232 | tf_op jit(solution)/shard_map/convert_element_type | solution.py:37
  174.9 2.6 broadcast.7.clone2
  177.4 211.0 %while.20 = (s32[]{:T(128)}, f32[4096,256]{0,1:T(8,128)}, s32[]{:T(128)}, s32[32]{0:T(128)S(1)}, bf16[32,8,128,128]{3,2,1,0:T(8,128)(2,1)}, /*index=5*/s32[32]{0...) while((s32[]{:T(128)}, f32[4096,256]{0,1:T(8,128)}, ...), condition=%wide.region_1.0_spmd, body=%wide.region_0.0_spmd.sunk | while | flops 67141648 | bytes 2097443 | solution.py:54
  181.8 1.4 fusion.23
  195.0 1.4 fusion.23
  214.7 1.4 fusion.23
  221.3 1.4 fusion.23
  313.3 1.4 fusion.23
  388.5 1.9 copy.14
  390.4 8.5 %reduce-scatter.3.cloned.1.call-done = f32[2048,256]{0,1:T(8,128)} async-done(((f32[4096,256]{0,1:T(8,128)}), f32[2048,256]{0,1:T(8,128)}) %reduce-scatter.3.cloned.1.call-update) | async-done | bytes 2097168 | tf_op jit(solution)/shard_map/reduce_scatter | solution.py:57
  398.9 5.6 add_divide_fusion.1
  404.6 151.1 %all-gather.5.cloned.1.call-done = f32[8192,256]{0,1:T(8,128)} async-done(((f32[2048,256]{0,1:T(8,128)}), f32[8192,256]{0,1:T(8,128)}) %all-gather.5.cloned.1.call-update) | async-done | bytes 8388624 | tf_op jit(solution)/shard_map/all_gather | solution.py:36
  555.6 9.0 %copy.12 = f32[8192,256]{1,0:T(8,128)} copy(f32[8192,256]{0,1:T(8,128)} %all-gather.5.cloned.1.call-done) | data formatting | bytes 16777216 | tf_op jit(solution)/shard_map/all_gather | solution.py:36
  564.6 13.6 %multiply_convert_fusion = bf16[8,8192,256]{2,1,0:T(8,128)(2,1)} fusion(f32[8192,256]{1,0:T(8,128)} %copy.12, f32[8,256]{1,0:T(8,128)S(1)} %bitcast.46), kind=kLoop, calls=%fused_computation.16 | loop fusion | flops 33554432 | bytes 41951232 | tf_op jit(solution)/shard_map/convert_element_type | solution.py:37
  578.2 2.6 broadcast.7.clone
  580.8 203.4 %while.21 = (s32[]{:T(128)}, f32[4096,256]{0,1:T(8,128)}, s32[]{:T(128)}, s32[32]{0:T(128)S(1)}, bf16[32,8,128,128]{3,2,1,0:T(8,128)(2,1)}, /*index=5*/s32[32]{0...) while((s32[]{:T(128)}, f32[4096,256]{0,1:T(8,128)}, ...), condition=%wide.region_4.0_spmd, body=%wide.region_3.0_spmd.sunk | while | flops 67141648 | bytes 2097443 | solution.py:54
  629.3 1.4 fusion.26
  724.3 1.4 fusion.26
  749.7 1.4 fusion.26
  762.3 1.4 fusion.26
  784.2 10.4 %reduce-scatter.5.cloned.1.call-done = f32[2048,256]{0,1:T(8,128)} async-done(((f32[4096,256]{0,1:T(8,128)}), f32[2048,256]{0,1:T(8,128)}) %reduce-scatter.5.cloned.1.call-update) | async-done | bytes 2097168 | tf_op jit(solution)/shard_map/reduce_scatter | solution.py:57
  794.6 4.1 add_divide_fusion
  798.7 2.9 copy.15
  (456 shorter events, 271.4 us)
Async XLA Ops:
  6.5 392.4 %copy-start = (f32[8,2048]{1,0:T(8,128)S(1)}, f32[8,2048]{1,0:T(8,128)}, u32[]{:S(2)}) copy-start(f32[8,2048]{1,0:T(8,128)} %param.15) | copy-start | bytes 196612
  6.5 154.8 %all-gather.3.cloned.1.call-start = ((), (), s32[]{:S(2)}) async-start(), calls=%async_computation.2 | async-start | bytes 10485760 | tf_op jit(solution)/shard_map/all_gather | solution.py:36
  7.3 391.7 %reduce-scatter.3.cloned.1.call-start = ((), (), s32[]{:S(2)}) async-start(), calls=%async_computation.3 | async-start | bytes 6291456 | tf_op jit(solution)/shard_map/reduce_scatter | solution.py:57
  174.9 2.6 copy-start.2
  174.9 2.6 copy-start.3
  388.5 167.2 %all-gather.5.cloned.1.call-start = ((), (), s32[]{:S(2)}) async-start(), calls=%async_computation.4 | async-start | bytes 10485760 | tf_op jit(solution)/shard_map/all_gather | solution.py:36
  404.5 390.1 %reduce-scatter.5.cloned.1.call-start = ((), (), s32[]{:S(2)}) async-start(), calls=%async_computation.5 | async-start | bytes 6291456 | tf_op jit(solution)/shard_map/reduce_scatter | solution.py:57
  794.6 7.0 copy-start.1
Sparse Core Ops, SparseCore 0:
  8.9 152.3 all-gather.2
  388.6 10.2 reduce-scatter.2
  404.7 150.9 all-gather.4
  784.3 10.2 reduce-scatter.4
where the time goes:
time: 813 us; the launch traced here: 808 us
  waiting for transfers between devices  324 us (40%)
  local copies, waits for them, and re-layouts  213 us (26%)
  loops' own time  132 us (16%)
  matrix products  93.9 us (12%)
  other arithmetic  31.2 us (4%)
  between operations  13.2 us (2%)
    all_gather x2, waiting for transfers between devices, per_device(): lax.all_gather(populations, 'col', axis=0, tiled=True)[None, :, :]  304 us
    another operation x2, loops' own time, per_device(): lax.fori_loop(0, live_slots, add_slot, jnp.zeros((row_devices * part_rows...  132 us
    dot_general x64, matrix products, slot_product(): jnp.einsum('kij,kjc->ic', blocks[slot], fetch(slot), preferred_element_ty...  87.5 us
    dynamic_slice x128, local copies, waits for them, and re-layouts, add_slot(): current = lax.dynamic_slice_in_dim(totals, row_start, block_size, 0)  64.9 us
    dynamic_update_slice x128, local copies, waits for them, and re-layouts, add_slot(): lax.dynamic_update_slice_in_dim(totals, current + slot_product(slot), row...  49.4 us
    dynamic_slice x64, local copies, waits for them, and re-layouts, fetch(): slot_cols[slot] * block_size  40.2 us
    dynamic_slice x64, local copies, waits for them, and re-layouts, add_slot(): row_start = slot_rows[slot] * block_size  40 us
    convert_element_type x2, other arithmetic, per_device(): weighted = (factors[:, None, :] * lax.all_gather(populations, 'col', axis...  27.1 us
  transfers between devices with their start and end apart: 4, of which 4 were waited for; matrix products, arithmetic and copies ran while one was open for 0% of the time, Pallas kernels for 0%

commit v1 on v0

v1 whole, which is shorter than its diff:
```python
import jax
import jax.numpy as jnp
from jax import lax
from jax.experimental import pallas as pl
from jax.experimental.pallas import tpu as pltpu
from jax.sharding import PartitionSpec as P

ITERS = 2


def slots_kernel(count_ref, cols_ref, dest_ref, rates_ref, held_ref, factors_ref, theirs_ref, mine_ref):
    basis = rates_ref.shape[1]
    depth = mine_ref.shape[0]
    theirs_ref[...] = jnp.zeros_like(theirs_ref)
    mine_ref[...] = jnp.zeros_like(mine_ref)

    def slot_step(slot, carry):
        block = held_ref[cols_ref[slot]]
        weighted = jnp.concatenate(
            [(factors_ref[k : k + 1, :] * block).astype(jnp.bfloat16) for k in range(basis)], axis=0
        )
        rates = jnp.concatenate([rates_ref[slot, k] for k in range(basis)], axis=1)
        product = jnp.dot(rates, weighted, preferred_element_type=jnp.float32)
        place = dest_ref[slot]

        @pl.when(place < depth)
        def _():
            mine_ref[place] += product

        @pl.when(place >= depth)
        def _():
            theirs_ref[place - depth] += product

        return carry

    lax.fori_loop(0, count_ref[0], slot_step, 0)


def slot_sums(count, cols, dest, rates, held, factors, depth):
    slots, basis, block, _ = rates.shape
    cells = factors.shape[1]
    smem = pl.BlockSpec(memory_space=pltpu.SMEM)
    vmem = pl.BlockSpec(memory_space=pltpu.VMEM)
    half = jax.ShapeDtypeStruct((depth, block, cells), jnp.float32)
    return pl.pallas_call(
        slots_kernel,
        out_shape=(half, half),
        in_specs=[smem, smem, smem, vmem, vmem, vmem],
        out_specs=(vmem, vmem),
        compiler_params=pltpu.CompilerParams(vmem_limit_bytes=40 * 1024 * 1024),
        cost_estimate=pl.CostEstimate(
            flops=2 * slots * basis * block * block * cells,
            bytes_accessed=rates.size * 2 + held.size * 4 + 2 * depth * block * cells * 4,
            transcendentals=0,
        ),
    )(count, cols, dest, rates, held, factors)


def per_device(
    populations,
    source,
    loss_rates,
    basis_table,
    temp_bins,
    rate_blocks,
    block_rows,
    block_cols,
    block_count,
):
    levels, cells = populations.shape
    bin_count = basis_table.shape[1]
    block = rate_blocks.shape[-1]
    per_piece = levels // block
    onehot = (temp_bins[None, :] == jnp.arange(bin_count, dtype=jnp.int32)[:, None]).astype(
        jnp.float32
    )
    factors = jnp.dot(basis_table, onehot, precision=lax.Precision.HIGHEST)
    denominator = jnp.einsum("kl,kc->lc", loss_rates, factors, precision=lax.Precision.HIGHEST)
    rates = rate_blocks[0, 0]
    rows = block_rows[0, 0]
    own = rows // per_piece == lax.axis_index("row")
    dest = rows % per_piece + jnp.where(own, 0, per_piece)
    for sweep in range(ITERS):
        held = lax.all_gather(populations, "col", axis=0, tiled=True).reshape(-1, block, cells)
        theirs, mine = slot_sums(
            block_count[0], block_cols[0, 0], dest, rates, held, factors, per_piece
        )
        arrived = lax.ppermute(theirs, "row", [(0, 1), (1, 0)])
        coupling = (mine + arrived).reshape(levels, cells)
        populations = (source + coupling) / denominator
    return populations


def solution(mesh):
    in_specs = (
        P(("row", "col"), "cell"),
        P(("row", "col"), "cell"),
        P(None, ("row", "col")),
        P(),
        P("cell"),
        P("row", "col", None, None, None, None),
        P("row", "col", None),
        P("row", "col", None),
        P("row", "col"),
    )
    out_specs = P(("row", "col"), "cell")
    return jax.shard_map(
        per_device, mesh=mesh, in_specs=in_specs, out_specs=out_specs, check_vma=False
    )
```

time: 813 us -> 389 us (0.48)
  local copies, waits for them, and re-layouts: 213 us -> 27.6 us
  loops' own time: 132 us -> 0 us
  matrix products: 93.9 us -> 3.28 us
  waiting for transfers between devices: 324 us -> 306 us
  other arithmetic: 31.2 us -> 13.4 us
  Pallas kernels: 0 us -> 15.2 us
  starting transfers between devices: 0.12 us -> 9.77 us
    dynamic_slice x256 -> x0, local copies, waits for them, and re-layouts: 145 us -> none  [the longest x128 64.9 us: add_slot(): current = lax.dynamic_slice_in_dim(totals, row_start, block_size, 0)]
    another operation x2 -> x0, loops' own time: 132 us -> none  [per_device(): lax.fori_loop(0, live_slots, add_slot, jnp.zeros((row_devices * part_rows...]
    dot_general x64 -> x0, matrix products: 87.5 us -> none  [slot_product(): jnp.einsum('kij,kjc->ic', blocks[slot], fetch(slot), preferred_element_ty...]
    dynamic_update_slice x128 -> x0, local copies, waits for them, and re-layouts: 49.4 us -> none  [add_slot(): lax.dynamic_update_slice_in_dim(totals, current + slot_product(slot), row...]
    convert_element_type x2 -> x0, other arithmetic: 27.1 us -> none  [per_device(): weighted = (factors[:, None, :] * lax.all_gather(populations, 'col', axis...]
    reduce_scatter x2 -> x0, waiting for transfers between devices: 18.9 us -> none  [per_device(): coupling = lax.psum_scatter(totals, 'row', scatter_dimension=0, tiled=True)]
    pallas_call x0 -> x2, Pallas kernels: none -> 15.2 us  [slot_sums(): pl.pallas_call(slots_kernel, out_shape=(half, half), in_specs=[smem, smem...]
    ppermute x0 -> x2, starting transfers between devices: none -> 9.69 us  [per_device(): arrived = lax.ppermute(theirs, 'row', [(0, 1), (1, 0)])]
  transfers between devices with their start and end apart: 4 -> 4, of which waited for: 4 -> 3; matrix products, arithmetic and copies ran while one was open for 0% -> 2% of each run, Pallas kernels for 0% -> 0%
where the time goes in v1:
time: 389 us
  waiting for transfers between devices  306 us (79%)
  local copies, waits for them, and re-layouts  27.6 us (7%)
  Pallas kernels  15.2 us (4%)
  between operations  14.1 us (4%)
  other arithmetic  13.4 us (3%)
  starting transfers between devices  9.77 us (3%)
    all_gather x2, waiting for transfers between devices, per_device(): lax.all_gather(populations, 'col', axis=0, tiled=True)  301 us
    pallas_call x2, Pallas kernels, slot_sums(): pl.pallas_call(slots_kernel, out_shape=(half, half), in_specs=[smem, smem...  15.2 us
    unnamed x19, local copies, waits for them, and re-layouts  9.7 us
    ppermute x2, starting transfers between devices, per_device(): arrived = lax.ppermute(theirs, 'row', [(0, 1), (1, 0)])  9.69 us
    all_gather x1, local copies, waits for them, and re-layouts, per_device(): lax.all_gather(populations, 'col', axis=0, tiled=True)  8.98 us
    div x2, other arithmetic, per_device(): populations = (source + coupling) / denominator  8.51 us
  transfers between devices with their start and end apart: 4, of which 3 were waited for; matrix products, arithmetic and copies ran while one was open for 2% of the time, Pallas kernels for 0%

profile of v1, /device:TPU:0, one launch (start us, length us, event | category | flops | bytes accessed | tf_op | source)
XLA Modules:
  0.0 389.0 jit_solution(7085036028080978531)
XLA Ops:
  6.5 0.0 all-gather.3.cloned.1.call-start
  6.6 0.7 all-gather.3.cloned.1.call-update
  7.3 0.0 all-gather.5.cloned.1.call-start
  8.0 0.1 fusion
  8.2 153.2 %all-gather.3.cloned.1.call-done = f32[8192,256]{1,0:T(8,128)} async-done(((f32[2048,256]{1,0:T(8,128)}), f32[8192,256]{1,0:T(8,128)}) %all-gather.3.cloned.1.call-update) | async-done | bytes 8388624 | tf_op jit(solution)/shard_map/all_gather | solution.py:84
  161.3 3.4 copy-done.2
  164.7 8.3 %shard_map.91 = (f32[16,128,256]{2,1,0:T(8,128)}, f32[16,128,256]{2,1,0:T(8,128)S(1)}) custom-call(s32[1]{0:T(128)} %bitcast.26.count_ref, s32[32]{0:T(128)S(1)} %bitcast.32, s32[32]{0:T(128)S(1)} %fusion.2.dest_ref, bf16[32,8,128,128]{3,2,1,0:T(8,128)(2,1)S(1)} %bitcast.28, f32[64,128,256]{2,1,0:T(8,128)} %bitcast.35, f32[8,256]{1,0:T(8,128)S(1)} %bitcast.30), custom_call_target="tpu_custom_call" | custom-call | flops 2147483648 | bytes 20971520 | tf_op jit(solution)/shard_map/pallas_call | solution.py:45
  173.0 4.8 %collective-permute-start = (f32[16,128,256]{2,1,0:T(8,128)}, f32[16,128,256]{2,1,0:T(8,128)}, u32[]{:S(2)}, u32[]{:S(2)}) collective-permute-start(f32[16,128,256]{2,1,0:T(8,128)} %get-tuple-element.10), channel_id=1, source_target_pairs={{0,16},{16,0},{1,17},{17,1},{2,18},{18,2},{3,19},{19,3},{4,20},{20... | collective-permute-start | bytes 6291464 | tf_op jit(solution)/shard_map/ppermute | solution.py:88
  177.8 2.9 copy.13
  180.7 3.2 convolution_bitcast_fusion
  183.9 3.3 add.24
  187.2 3.1 copy.11
  190.3 4.3 %add_divide_fusion.1 = f32[2048,256]{0,1:T(8,128)} fusion(f32[2048,256]{0,1:T(8,128)} %convolution_bitcast_fusion, f32[2048,256]{0,1:T(8,128)S(1)} %copy-done.5, f32[2048,256]{0,1:T(8,128)} %copy.11), kind=kLoop, calls=%fused_computation.2 | loop fusion | flops 1048576 | bytes 8388608 | tf_op jit(solution)/shard_map/div | solution.py:90
  194.5 0.0 all-gather.5.cloned.1.call-update
  194.6 147.9 %all-gather.5.cloned.1.call-done = f32[8192,256]{0,1:T(8,128)} async-done(((f32[2048,256]{0,1:T(8,128)}), f32[8192,256]{0,1:T(8,128)}) %all-gather.5.cloned.1.call-update) | async-done | bytes 8388624 | tf_op jit(solution)/shard_map/all_gather | solution.py:84
  342.5 9.0 %copy.12 = f32[8192,256]{1,0:T(8,128)} copy(f32[8192,256]{0,1:T(8,128)} %all-gather.5.cloned.1.call-done) | data formatting | bytes 16777216 | tf_op jit(solution)/shard_map/all_gather | solution.py:84
  351.5 3.4 copy-done.3
  354.9 6.9 %shard_map.92 = (f32[16,128,256]{2,1,0:T(8,128)S(1)}, f32[16,128,256]{2,1,0:T(8,128)S(1)}) custom-call(s32[1]{0:T(128)} %bitcast.27.count_ref, s32[32]{0:T(128)S(1)} %bitcast.33, s32[32]{0:T(128)S(1)} %fusion.2.dest_ref, bf16[32,8,128,128]{3,2,1,0:T(8,128)(2,1)S(1)} %bitcast.29, f32[64,128,256]{2,1,0:T(8,128)} %bitcast.34, f32[8,256]{1,0:T(8,128)S(1)} %bitcast.31), custom_call_target="tpu_custom_call" | custom-call | flops 2147483648 | bytes 20971520 | tf_op jit(solution)/shard_map/pallas_call | solution.py:45
  361.8 4.9 %collective-permute-start.1 = (f32[16,128,256]{2,1,0:T(8,128)S(1)}, f32[16,128,256]{2,1,0:T(8,128)S(1)}, u32[]{:S(2)}, u32[]{:S(2)}) collective-permute-start(f32[16,128,256]{2,1,0:T(8,128)S(1)} %get-tuple-element.12), channel_id=1, source_target_pairs={{0,16},{16,0},{1,17},{17,1},{2,18},{18,2},{3,19},{19,3},{4,20},{20... | collective-permute-start | bytes 6291464 | tf_op jit(solution)/shard_map/ppermute | solution.py:88
  366.6 3.8 collective-permute-done.1
  370.4 1.7 add.26
  372.1 2.9 copy.14
  375.0 4.2 %add_divide_fusion = f32[2048,256]{0,1:T(8,128)} fusion(f32[2048,256]{0,1:T(8,128)} %convolution_bitcast_fusion, f32[2048,256]{0,1:T(8,128)S(1)} %copy-done.5, f32[2048,256]{0,1:T(8,128)} %copy.14), kind=kLoop, calls=%fused_computation.1 | loop fusion | flops 1048576 | bytes 8388608 | tf_op jit(solution)/shard_map/div | solution.py:90
  379.2 2.9 copy.15
  (18 shorter events, 0.0 us)
Async XLA Ops:
  6.5 174.2 %copy-start = (f32[8,2048]{1,0:T(8,128)S(1)}, f32[8,2048]{1,0:T(8,128)}, u32[]{:S(2)}) copy-start(f32[8,2048]{1,0:T(8,128)} %param.11) | copy-start | bytes 196612
  6.5 1.4 copy-start.8
  6.5 1.5 copy-start.7
  6.5 1.5 copy-start.6
  6.5 154.8 %copy-start.4 = (s32[1,1,32]{2,1,0:T(1,128)S(1)}, s32[1,1,32]{2,1,0:T(1,128)}, u32[]{:S(2)}) copy-start(s32[1,1,32]{2,1,0:T(1,128)} %param.16) | copy-start | bytes 388
  6.5 154.8 %all-gather.3.cloned.1.call-start = ((), (), s32[]{:S(2)}) async-start(), calls=%async_computation | async-start | bytes 10485760 | tf_op jit(solution)/shard_map/all_gather | solution.py:84
  7.3 335.2 %all-gather.5.cloned.1.call-start = ((), (), s32[]{:S(2)}) async-start(), calls=%async_computation.1 | async-start | bytes 10485760 | tf_op jit(solution)/shard_map/all_gather | solution.py:84
  161.3 3.4 copy-start.2
  173.0 10.9 %collective-permute-start = (f32[16,128,256]{2,1,0:T(8,128)}, f32[16,128,256]{2,1,0:T(8,128)}, u32[]{:S(2)}, u32[]{:S(2)}) collective-permute-start(f32[16,128,256]{2,1,0:T(8,128)} %get-tuple-element.10), channel_id=1, source_target_pairs={{0,16},{16,0},{1,17},{17,1},{2,18},{18,2},{3,19},{19,3},{4,20},{20... | collective-permute-start | bytes 6291464 | tf_op jit(solution)/shard_map/ppermute | solution.py:88
  187.2 3.1 copy-start.5
  351.5 3.4 copy-start.3
  361.8 8.7 %collective-permute-start.1 = (f32[16,128,256]{2,1,0:T(8,128)S(1)}, f32[16,128,256]{2,1,0:T(8,128)S(1)}, u32[]{:S(2)}, u32[]{:S(2)}) collective-permute-start(f32[16,128,256]{2,1,0:T(8,128)S(1)} %get-tuple-element.12), channel_id=1, source_target_pairs={{0,16},{16,0},{1,17},{17,1},{2,18},{18,2},{3,19},{19,3},{4,20},{20... | collective-permute-start | bytes 6291464 | tf_op jit(solution)/shard_map/ppermute | solution.py:88
  375.0 7.1 %copy-start.1 = (f32[8,2048]{1,0:T(8,128)S(1)}, f32[8,2048]{1,0:T(8,128)}, u32[]{:S(2)}) copy-start(f32[8,2048]{1,0:T(8,128)} %param.11) | copy-start | bytes 196612
Sparse Core Ops, SparseCore 0:
  9.0 152.3 all-gather.2
  194.7 147.7 all-gather.4
